TPU v7x, 32 devices: a whole 2x2x4 slice. The times are simulated.
32 devices in a mesh: groups: 2 (over y), seq: 16 (over z, x, core).
Axes of the slice: x: 2, y: 2, z: 4, core: 2. Of those that a mesh axis runs over, the one named last changes fastest.
Arguments:
- inputs: bfloat16 [32768, 512], P(('groups', 'seq')), parts along dimension 0, may hold values from -36 to 36
- norm_gain: float32 [512], replicated, may hold values from 0.5 to 1.5
- dilated_weight: bfloat16 [3, 512, 512], replicated, may hold values from -0.15625 to 0.15625
- local_weight: bfloat16 [5, 512, 512], replicated, may hold values from -0.125 to 0.125
- cotangent: bfloat16 [32768, 512], P(('groups', 'seq')), parts along dimension 0, may hold values from -6 to 6
Outputs:
- block_out: bfloat16 [32768, 512], P(('groups', 'seq')), parts along dimension 0
- input_grad: bfloat16 [32768, 512], P(('groups', 'seq')), parts along dimension 0
- grad_dilated: float32 [3072, 512], P(('groups', 'seq')), parts along dimension 0
- grad_local: float32 [5120, 512], P(('groups', 'seq')), parts along dimension 0
There are 2 independent parts, one for each index of `groups`. A program takes and returns all parts, laid end to end along the dimension named above; an argument that names none is the same for every part. Nothing has to cross between parts.
All inputs are finite; a program needn't handle non-finite values.
Results may differ from a plain program's by a relative error of at most 0.0053.
Values may be sent and summed in bfloat16 or wider, within the bound.
A program may use at most 128 MiB of HBM per device.

v0:
```python
import math

import jax
import jax.numpy as jnp
from jax import lax
from jax.sharding import PartitionSpec as P

DILATION_BINS = 8192


def from_behind(x, axis, by):
    devices = lax.axis_size(axis)
    pairs = [(i, i + by) for i in range(devices) if 0 <= i + by < devices]
    return lax.ppermute(x, axis, pairs)


def with_halo(block, sides, width):
    for axis, dim in sides:
        count = lax.axis_size(axis)
        forward = [(i, i + 1) for i in range(count - 1)]
        backward = [(target, source) for source, target in forward]
        low = lax.ppermute(
            lax.slice_in_dim(block, block.shape[dim] - width, None, axis=dim), axis, forward
        )
        high = lax.ppermute(lax.slice_in_dim(block, 0, width, axis=dim), axis, backward)
        block = jnp.concatenate([low, block, high], axis=dim)
    return block


def prepare(values, gain):
    meansq = jnp.mean(values * values, axis=-1, keepdims=True) + 1e-06
    return jax.nn.gelu(values * lax.rsqrt(meansq) * gain, approximate=True)


def transposed_term(left, right, scale):
    product = lax.dot_general(
        left, right, (((0,), (0,)), ((), ())), preferred_element_type=jnp.float32
    )
    return product * scale


def on_device(inputs, norm_gain, dilated_weight, local_weight, cotangent):
    sequence_rows, width = inputs.shape
    devices = lax.axis_size("seq")
    dilation_stride = DILATION_BINS // sequence_rows
    scale = 1.0 / math.sqrt(sequence_rows * devices)
    values = inputs.astype(jnp.float32)
    act_f, pull = jax.vjp(lambda v: prepare(v, norm_gain), values)
    activation_input = act_f.astype(jnp.bfloat16)
    earlier = from_behind(activation_input, "seq", dilation_stride)
    later = from_behind(activation_input, "seq", -dilation_stride)
    gathered_activation = jnp.concatenate([earlier, activation_input, later], axis=1)
    mid = jnp.dot(
        gathered_activation,
        dilated_weight.reshape(3 * width, width),
        preferred_element_type=jnp.float32,
    )
    hid_f, gelu_pull = jax.vjp(lambda m: jax.nn.gelu(m, approximate=True), mid)
    hidden = hid_f.astype(jnp.bfloat16)
    padded = with_halo(hidden, (("seq", 0),), 2)
    hid_all = jnp.concatenate([padded[j : j + sequence_rows] for j in range(5)], axis=1)
    out = jnp.dot(
        hid_all, local_weight.reshape(5 * width, width), preferred_element_type=jnp.float32
    )
    block_out = (values + out).astype(jnp.bfloat16)
    cot_padded = with_halo(cotangent, (("seq", 0),), 2)
    cot_all = jnp.concatenate([cot_padded[4 - j : 4 - j + sequence_rows] for j in range(5)], axis=1)
    local_t = jnp.transpose(local_weight, (0, 2, 1)).reshape(5 * width, width)
    d_hidden = jnp.dot(cot_all, local_t, preferred_element_type=jnp.float32)
    middle_gradient = gelu_pull(d_hidden)[0].astype(jnp.bfloat16)
    grad_local = lax.psum_scatter(
        transposed_term(hid_all, cotangent, scale), "seq", scatter_dimension=0, tiled=True
    )
    dilated_t = jnp.transpose(dilated_weight, (0, 2, 1))
    first_part = jnp.dot(middle_gradient, dilated_t[0], preferred_element_type=jnp.float32)
    last_part = jnp.dot(middle_gradient, dilated_t[2], preferred_element_type=jnp.float32)
    centre_part = jnp.dot(middle_gradient, dilated_t[1], preferred_element_type=jnp.float32)
    moved_first = from_behind(first_part.astype(jnp.bfloat16), "seq", -dilation_stride).astype(
        first_part.dtype
    )
    moved_last = from_behind(last_part.astype(jnp.bfloat16), "seq", dilation_stride).astype(
        last_part.dtype
    )
    d_act = moved_first + centre_part + moved_last
    grad_dilated = lax.psum_scatter(
        transposed_term(gathered_activation, middle_gradient, scale),
        "seq",
        scatter_dimension=0,
        tiled=True,
    )
    input_grad = (cotangent.astype(jnp.float32) + pull(d_act)[0]).astype(jnp.bfloat16)
    return (block_out, input_grad, grad_dilated, grad_local)


def solution(mesh):
    return jax.shard_map(
        on_device,
        mesh=mesh,
        in_specs=(P(("groups", "seq"), None), P(), P(), P(), P(("groups", "seq"), None)),
        out_specs=(
            P(("groups", "seq"), None),
            P(("groups", "seq"), None),
            P(("groups", "seq"), None),
            P(("groups", "seq"), None),
        ),
        check_vma=False,
    )
```

profile of v0, /device:TPU:3, one launch (start us, length us, event | category | flops | bytes accessed | tf_op | source)
XLA Modules:
  0.0 260.2 jit_solution(12290109310035369557)
XLA Ops:
  7.2 1.6 fusion.16
  8.8 2.1 fusion.22
  11.0 1.3 collective-permute-start.1
  12.3 6.8 %collective-permute-start = (bf16[1024,512]{1,0:T(8,128)(2,1)S(1)}, bf16[1024,512]{1,0:T(8,128)(2,1)}, u32[]{:S(2)}, u32[]{:S(2)}) collective-permute-start(bf16[1024,512]{1,0:T(8,128)(2,1)S(1)} %fusion.22), channel_id=1, source_target_pairs={{0,8},{1,9},{2,10},{3,11},{4,12},{5,13},{6,14},{7,15},{16,24},{17,... | collective-permute-start | bytes 3145736 | tf_op jit(solution)/shard_map/ppermute | solution.py:14
  19.1 3.1 %collective-permute-start.4 = (bf16[2,512]{1,0:T(2,128)(2,1)S(1)}, bf16[2,512]{1,0:T(2,128)(2,1)S(1)}, u32[]{:S(2)}, u32[]{:S(2)}) collective-permute-start(bf16[2,512]{1,0:T(2,128)(2,1)S(1)} %get-tuple-element.7), channel_id=1, source_target_pairs={{1,0},{2,1},{3,2},{4,3},{5,4},{6,5},{7,6},{8,7},{9,8},{10,9},{11,1... | collective-permute-start | bytes 6152 | tf_op jit(solution)/shard_map/ppermute | solution.py:25
  22.3 3.3 %collective-permute-start.5 = (bf16[2,512]{1,0:T(2,128)(2,1)S(1)}, bf16[2,512]{1,0:T(2,128)(2,1)S(1)}, u32[]{:S(2)}, u32[]{:S(2)}) collective-permute-start(bf16[2,512]{1,0:T(2,128)(2,1)S(1)} %get-tuple-element.6), channel_id=1, source_target_pairs={{0,1},{1,2},{2,3},{3,4},{4,5},{5,6},{6,7},{7,8},{8,9},{9,10},{10,1... | collective-permute-start | bytes 6152 | tf_op jit(solution)/shard_map/ppermute | solution.py:22
  25.7 4.4 %copy.10 = bf16[5,512,512]{1,2,0:T(8,128)(2,1)} copy(bf16[5,512,512]{2,1,0:T(8,128)(2,1)} %param.8) | data formatting | bytes 5242880 | tf_op args[3]
  30.7 9.1 %collective-permute-done.5 = bf16[2,512]{1,0:T(2,128)(2,1)S(1)} collective-permute-done((bf16[2,512]{1,0:T(2,128)(2,1)S(1)}, bf16[2,512]{1,0:T(2,128)(2,1)S(1)}, u32[]{:S(2)}, u32[]{:S(2)}) %collective-permute-start.5) | collective-permute-done | bytes 2080 | tf_op jit(solution)/shard_map/ppermute | solution.py:22
  40.0 0.2 fusion.32
  40.2 2.9 %fusion.41 = f32[1024,512]{1,0:T(8,128)S(1)} fusion(bf16[1024,2560]{1,0:T(8,128)(2,1)S(1)} %fusion.32, bf16[2560,512]{1,0:T(8,128)(2,1)S(1)} %bitcast.31), kind=kOutput, calls=%fused_computation.77 | convolution fusion | flops 2684354560 | bytes 9961472 | tf_op jit(solution)/shard_map/dot_general | solution.py:69
  43.1 17.3 %collective-permute-done.1 = bf16[1024,512]{1,0:T(8,128)(2,1)} collective-permute-done((bf16[1024,512]{1,0:T(8,128)(2,1)S(1)}, bf16[1024,512]{1,0:T(8,128)(2,1)}, u32[]{:S(2)}, u32[]{:S(2)}) %collective-permute-start.1) | collective-permute-done | bytes 1048608 | tf_op jit(solution)/shard_map/ppermute | solution.py:14
  60.4 5.6 %fusion.13 = (bf16[1024,512]{1,0:T(8,128)(2,1)}, bf16[1024,512]{1,0:T(8,128)(2,1)S(1)}) fusion(f32[1024,512]{1,0:T(8,128)S(1)} %fusion.41, bf16[1536,512]{1,0:T(8,128)(2,1)S(1)} %bitcast.32, bf16[1024,512]{1,0:T(8,128)(2,1)} %collective-permute-done.1, bf16[1024,512]{1,0:T(8,128)(2,1)S(1)} %fusion.22, bf16[1024,512]{1,0:T(8,128)(2,1)} %collective-permute-done), kind=kOutput, calls=%fused_computation.26 | convolution fusion | flops 1631584256 | bytes 8912896 | tf_op jit(solution)/shard_map/dot_general | solution.py:53
  66.0 5.5 %convolution_multiply_fusion.1 = f32[1536,512]{1,0:T(8,128)} fusion(bf16[1024,512]{1,0:T(8,128)(2,1)} %get-tuple-element.4, bf16[1024,512]{1,0:T(8,128)(2,1)} %collective-permute-done.1, bf16[1024,512]{1,0:T(8,128)(2,1)S(1)} %fusion.22, bf16[1024,512]{1,0:T(8,128)(2,1)} %collective-permute-done), kind=kOutput, calls=%fused_computation.6 | convolution fusion | flops 1620836352 | bytes 7340032 | tf_op jit(solution)/shard_map/dot_general | solution.py:36
  71.5 5.8 %collective-permute-start.2 = (bf16[2,512]{1,0:T(2,128)(2,1)S(1)}, bf16[2,512]{1,0:T(2,128)(2,1)S(1)}, u32[]{:S(2)}, u32[]{:S(2)}) collective-permute-start(bf16[2,512]{1,0:T(2,128)(2,1)S(1)} %get-tuple-element.9), channel_id=1, source_target_pairs={{0,1},{1,2},{2,3},{3,4},{4,5},{5,6},{6,7},{7,8},{8,9},{9,10},{10,1... | collective-permute-start | bytes 6152 | tf_op jit(solution)/shard_map/ppermute | solution.py:22
  77.4 2.1 collective-permute-start.3
  79.5 1.3 fusion.31
  80.8 1.3 fusion.34
  82.0 1.2 constant_dynamic-update-slice_fusion
  83.3 1.3 fusion.29
  84.5 1.3 fusion.33
  85.8 7.5 %convolution_multiply_fusion = f32[2560,512]{1,0:T(8,128)} fusion(bf16[1024,2560]{1,0:T(8,128)(2,1)} %fusion.33, bf16[1024,512]{1,0:T(8,128)(2,1)S(1)} %copy-done), kind=kOutput, calls=%fused_computation | convolution fusion | flops 2685665280 | bytes 11534336 | tf_op jit(solution)/shard_map/dot_general | solution.py:36
  93.3 1.5 copy-done.6
  94.8 2.2 convolution_convert_fusion
  97.0 2.1 convolution_convert_fusion.1
  99.1 5.1 %collective-permute-start.7 = (bf16[1024,512]{1,0:T(8,128)(2,1)S(1)}, bf16[1024,512]{1,0:T(8,128)(2,1)S(1)}, u32[]{:S(2)}, u32[]{:S(2)}) collective-permute-start(bf16[1024,512]{1,0:T(8,128)(2,1)S(1)} %convolution_convert_fusion), channel_id=1, source_target_pairs={{0,8},{1,9},{2,10},{3,11},{4,12},{5,13},{6,14},{7,15},{16,24},{17,... | collective-permute-start | bytes 3145736 | tf_op jit(solution)/shard_map/ppermute | solution.py:14
  104.2 1.3 collective-permute-start.6
  105.5 6.4 %fusion.23 = bf16[1024,512]{1,0:T(8,128)(2,1)} fusion(bf16[1024,512]{1,0:T(8,128)(2,1)S(1)} %copy-done.1, bf16[1024,2560]{1,0:T(8,128)(2,1)} %fusion.33, bf16[2560,512]{1,0:T(8,128)(2,1)S(1)} %bitcast.30), kind=kOutput, calls=%fused_computation.36 | convolution fusion | flops 2685927424 | bytes 9961472 | tf_op jit(solution)/shard_map/dot_general | solution.py:62
  111.9 21.2 %collective-permute-done.7 = bf16[1024,512]{1,0:T(8,128)(2,1)S(1)} collective-permute-done((bf16[1024,512]{1,0:T(8,128)(2,1)S(1)}, bf16[1024,512]{1,0:T(8,128)(2,1)S(1)}, u32[]{:S(2)}, u32[]{:S(2)}) %collective-permute-start.7) | collective-permute-done | bytes 1048608 | tf_op jit(solution)/shard_map/ppermute | solution.py:14
  133.1 38.1 %collective-permute-done.6 = bf16[1024,512]{1,0:T(8,128)(2,1)S(1)} collective-permute-done((bf16[1024,512]{1,0:T(8,128)(2,1)S(1)}, bf16[1024,512]{1,0:T(8,128)(2,1)S(1)}, u32[]{:S(2)}, u32[]{:S(2)}) %collective-permute-start.6) | collective-permute-done | bytes 1048608 | tf_op jit(solution)/shard_map/ppermute | solution.py:14
  171.2 4.0 %fusion.24 = (f32[1024]{0:T(1024)S(1)}, f32[1024,512]{1,0:T(8,128)S(1)}) fusion(bf16[1024,512]{1,0:T(8,128)(2,1)S(1)} %copy-done.1, f32[512]{0:T(512)S(1)} %copy-done.4, f32[1024]{0:T(1024)S(1)} %fusion.36, bf16[1024,512]{1,0:T(8,128)(2,1)S(1)} %collective-permute-done.7, bf16[1024,512]{1,0:T(8,128)(2,1)} %get-tuple-element.4, ...), kind=kOutput, calls=%fused_computation.37 | convolution fusion | flops 552074240 | bytes 6825984 | tf_op jit(solution)/shard_map/dot_general | solution.py:77
  175.3 1.6 fusion.15
  176.8 76.5 %reduce-scatter.5.cloned.1.call-done = f32[160,512]{1,0:T(8,128)} async-done(((f32[2560,512]{1,0:T(8,128)}), f32[160,512]{1,0:T(8,128)}) %reduce-scatter.5.cloned.1.call-update) | async-done | bytes 327696 | tf_op jit(solution)/shard_map/reduce_scatter | solution.py:71
  (32 shorter events, 1.1 us)
Async XLA Ops:
  7.2 11.9 %copy-start = (bf16[1024,512]{1,0:T(8,128)(2,1)S(1)}, bf16[1024,512]{1,0:T(8,128)(2,1)}, u32[]{:S(2)}) copy-start(bf16[1024,512]{1,0:T(8,128)(2,1)} %param.9) | copy-start | bytes 3145732
  7.2 169.7 %reduce-scatter.3.cloned.1.call-start = ((), (), s32[]{:S(2)}) async-start(), calls=%async_computation.2 | async-start | bytes 3342336 | tf_op jit(solution)/shard_map/reduce_scatter | solution.py:85
  11.0 49.4 %collective-permute-start.1 = (bf16[1024,512]{1,0:T(8,128)(2,1)S(1)}, bf16[1024,512]{1,0:T(8,128)(2,1)}, u32[]{:S(2)}, u32[]{:S(2)}) collective-permute-start(bf16[1024,512]{1,0:T(8,128)(2,1)S(1)} %fusion.22), channel_id=1, source_target_pairs={{8,0},{9,1},{10,2},{11,3},{12,4},{13,5},{14,6},{15,7},{24,16},{25,... | collective-permute-start | bytes 3145736 | tf_op jit(solution)/shard_map/ppermute | solution.py:14
  12.3 48.1 %collective-permute-start = (bf16[1024,512]{1,0:T(8,128)(2,1)S(1)}, bf16[1024,512]{1,0:T(8,128)(2,1)}, u32[]{:S(2)}, u32[]{:S(2)}) collective-permute-start(bf16[1024,512]{1,0:T(8,128)(2,1)S(1)} %fusion.22), channel_id=1, source_target_pairs={{0,8},{1,9},{2,10},{3,11},{4,12},{5,13},{6,14},{7,15},{16,24},{17,... | collective-permute-start | bytes 3145736 | tf_op jit(solution)/shard_map/ppermute | solution.py:14
  19.1 10.9 %collective-permute-start.4 = (bf16[2,512]{1,0:T(2,128)(2,1)S(1)}, bf16[2,512]{1,0:T(2,128)(2,1)S(1)}, u32[]{:S(2)}, u32[]{:S(2)}) collective-permute-start(bf16[2,512]{1,0:T(2,128)(2,1)S(1)} %get-tuple-element.7), channel_id=1, source_target_pairs={{1,0},{2,1},{3,2},{4,3},{5,4},{6,5},{7,6},{8,7},{9,8},{10,9},{11,1... | collective-permute-start | bytes 6152 | tf_op jit(solution)/shard_map/ppermute | solution.py:25
  22.3 17.4 %collective-permute-start.5 = (bf16[2,512]{1,0:T(2,128)(2,1)S(1)}, bf16[2,512]{1,0:T(2,128)(2,1)S(1)}, u32[]{:S(2)}, u32[]{:S(2)}) collective-permute-start(bf16[2,512]{1,0:T(2,128)(2,1)S(1)} %get-tuple-element.6), channel_id=1, source_target_pairs={{0,1},{1,2},{2,3},{3,4},{4,5},{5,6},{6,7},{7,8},{8,9},{9,10},{10,1... | collective-permute-start | bytes 6152 | tf_op jit(solution)/shard_map/ppermute | solution.py:22
  30.6 9.6 %copy-start.3 = (bf16[5,512,512]{1,2,0:T(8,128)(2,1)S(1)}, bf16[5,512,512]{1,2,0:T(8,128)(2,1)}, u32[]{:S(2)}) copy-start(bf16[5,512,512]{1,2,0:T(8,128)(2,1)} %copy.10) | copy-start | bytes 7864324
  40.2 20.2 %copy-start.5 = (bf16[3,512,512]{2,1,0:T(8,128)(2,1)S(1)}, bf16[3,512,512]{2,1,0:T(8,128)(2,1)}, u32[]{:S(2)}) copy-start(bf16[3,512,512]{2,1,0:T(8,128)(2,1)} %param.7) | copy-start | bytes 4718596
  71.4 181.9 %reduce-scatter.5.cloned.1.call-start = ((), (), s32[]{:S(2)}) async-start(), calls=%async_computation.3 | async-start | bytes 5570560 | tf_op jit(solution)/shard_map/reduce_scatter | solution.py:71
  71.5 8.0 %collective-permute-start.2 = (bf16[2,512]{1,0:T(2,128)(2,1)S(1)}, bf16[2,512]{1,0:T(2,128)(2,1)S(1)}, u32[]{:S(2)}, u32[]{:S(2)}) collective-permute-start(bf16[2,512]{1,0:T(2,128)(2,1)S(1)} %get-tuple-element.9), channel_id=1, source_target_pairs={{0,1},{1,2},{2,3},{3,4},{4,5},{5,6},{6,7},{7,8},{8,9},{9,10},{10,1... | collective-permute-start | bytes 6152 | tf_op jit(solution)/shard_map/ppermute | solution.py:22
  77.4 5.9 %collective-permute-start.3 = (bf16[2,512]{1,0:T(2,128)(2,1)S(1)}, bf16[2,512]{1,0:T(2,128)(2,1)S(1)}, u32[]{:S(2)}, u32[]{:S(2)}) collective-permute-start(bf16[2,512]{1,0:T(2,128)(2,1)S(1)} %get-tuple-element.8), channel_id=1, source_target_pairs={{1,0},{2,1},{3,2},{4,3},{5,4},{6,5},{7,6},{8,7},{9,8},{10,9},{11,1... | collective-permute-start | bytes 6152 | tf_op jit(solution)/shard_map/ppermute | solution.py:25
  93.3 1.5 copy-start.6
  94.8 10.7 %copy-start.2 = (bf16[5,512,512]{2,1,0:T(8,128)(2,1)S(1)}, bf16[5,512,512]{2,1,0:T(8,128)(2,1)}, u32[]{:S(2)}) copy-start(bf16[5,512,512]{2,1,0:T(8,128)(2,1)} %param.8) | copy-start | bytes 7864324
  97.0 8.5 %copy-start.1 = (bf16[1024,512]{1,0:T(8,128)(2,1)S(1)}, bf16[1024,512]{1,0:T(8,128)(2,1)}, u32[]{:S(2)}) copy-start(bf16[1024,512]{1,0:T(8,128)(2,1)} %param.5) | copy-start | bytes 3145732
  99.1 34.0 %collective-permute-start.7 = (bf16[1024,512]{1,0:T(8,128)(2,1)S(1)}, bf16[1024,512]{1,0:T(8,128)(2,1)S(1)}, u32[]{:S(2)}, u32[]{:S(2)}) collective-permute-start(bf16[1024,512]{1,0:T(8,128)(2,1)S(1)} %convolution_convert_fusion), channel_id=1, source_target_pairs={{0,8},{1,9},{2,10},{3,11},{4,12},{5,13},{6,14},{7,15},{16,24},{17,... | collective-permute-start | bytes 3145736 | tf_op jit(solution)/shard_map/ppermute | solution.py:14
  104.2 67.0 %collective-permute-start.6 = (bf16[1024,512]{1,0:T(8,128)(2,1)S(1)}, bf16[1024,512]{1,0:T(8,128)(2,1)S(1)}, u32[]{:S(2)}, u32[]{:S(2)}) collective-permute-start(bf16[1024,512]{1,0:T(8,128)(2,1)S(1)} %convolution_convert_fusion.1), channel_id=1, source_target_pairs={{8,0},{9,1},{10,2},{11,3},{12,4},{13,5},{14,6},{15,7},{24,16},{25,... | collective-permute-start | bytes 3145736 | tf_op jit(solution)/shard_map/ppermute | solution.py:14
  105.5 65.7 %copy-start.4 = (f32[512]{0:T(512)S(1)}, f32[512]{0:T(512)}, u32[]{:S(2)}) copy-start(f32[512]{0:T(512)} %param.6) | copy-start | bytes 6148
Sparse Core Ops, SparseCore 0:
  71.6 99.5 reduce-scatter.2
  175.5 77.7 reduce-scatter.4
where the time goes:
time: 263 us; the launch traced here: 260 us
  waiting for transfers between devices  162 us (62%)
  matrix products  36 us (14%)
  starting transfers between devices  29 us (11%)
  between operations  14.3 us (5%)
  other arithmetic  10.9 us (4%)
  local copies, waits for them, and re-layouts  7.74 us (3%)
    ppermute x4, waiting for transfers between devices, from_behind(): return lax.ppermute(x, axis, pairs)  76.6 us
    reduce_scatter x1, waiting for transfers between devices, on_device(): lax.psum_scatter(transposed_term(hid_all, cotangent, scale), 'seq', scatt...  76.5 us
    ppermute x4, starting transfers between devices, from_behind(): return lax.ppermute(x, axis, pairs)  14.5 us
    dot_general x2, matrix products, transposed_term(): lax.dot_general(left, right, (((0,), (0,)), ((), ())), preferred_element_...  12.9 us
    ppermute x2, starting transfers between devices, with_halo(): lax.ppermute(lax.slice_in_dim(block, block.shape[dim] - width, None, axis...  9.16 us
    ppermute x2, waiting for transfers between devices, with_halo(): lax.ppermute(lax.slice_in_dim(block, block.shape[dim] - width, None, axis...  9.05 us
    unnamed x20, local copies, waits for them, and re-layouts  7.72 us
    dot_general x1, matrix products, on_device(): jnp.dot(hid_all, local_weight.reshape(5 * width, width), preferred_elemen...  6.39 us
  transfers between devices with their start and end apart: 10, of which 5 were waited for; matrix products, arithmetic and copies ran while one was open for 15% of the time, Pallas kernels for 0%

commit v1 on v0

--- a/solution.py
+++ b/solution.py
@@ -1,11 +1,22 @@
+import functools
+import itertools
 import math
 
 import jax
 import jax.numpy as jnp
 from jax import lax
+from jax.experimental import pallas as pl
+from jax.experimental.pallas import tpu as pltpu
 from jax.sharding import PartitionSpec as P
 
 DILATION_BINS = 8192
+MESH = pl.DeviceIdType.MESH
+GELU_A = 0.7978845608028654
+GELU_B = 0.044715
+CHUNK = 128
+PAD = 16
+F32 = jnp.float32
+BF16 = jnp.bfloat16
 
 
 def from_behind(x, axis, by):
@@ -92,9 +103,353 @@
     return (block_out, input_grad, grad_dilated, grad_local)
 
 
+def gelu_and_slope(u):
+    t = jnp.tanh(GELU_A * (u + GELU_B * (u * u * u)))
+    half = 0.5 * (1.0 + t)
+    slope = half + 0.5 * u * (1.0 - t * t) * (GELU_A * (1.0 + 3.0 * GELU_B * (u * u)))
+    return u * half, slope
+
+
+def dot(x, w):
+    return jnp.dot(x, w, preferred_element_type=F32)
+
+
+def dot_t(x, w):
+    return lax.dot_general(x, w, (((1,), (1,)), ((), ())), preferred_element_type=F32)
+
+
+def bit_of(index, bit):
+    return lax.rem(lax.div(index, bit), 2)
+
+
+def across(index, bit):
+    return index + bit - 2 * bit * bit_of(index, bit)
+
+
+class HalvingSum:
+    def __init__(self, me, order, rows, acc, stage, recv, out, send_sem, recv_sem, scale):
+        self.me, self.order, self.rows, self.acc = me, order, rows, acc
+        self.stage, self.recv, self.out = stage, recv, out
+        self.send_sem, self.recv_sem, self.scale = send_sem, recv_sem, scale
+        self.base = [0]
+        for k in range(len(order)):
+            self.base.append(self.base[-1] + 2 ** (len(order) - 1 - k))
+
+    def combos(self, k):
+        return list(itertools.product((1, 0), repeat=len(self.order) - 1 - k))
+
+    def copy(self, k, slot):
+        s = self.base[k] + slot
+        return pltpu.make_async_remote_copy(
+            src_ref=self.stage.at[s],
+            dst_ref=self.recv.at[s],
+            send_sem=self.send_sem.at[s],
+            recv_sem=self.recv_sem.at[s],
+            device_id={"seq": across(self.me, self.order[k])},
+            device_id_type=MESH,
+        )
+
+    def block(self, flips):
+        index = 0
+        for bit, flip in zip(self.order, flips):
+            mine = bit_of(self.me, bit)
+            index = index + bit * (1 - mine if flip else mine)
+        return pl.ds(pl.multiple_of(index * self.rows, 16), self.rows)
+
+    def begin(self):
+        for slot, rel in enumerate(self.combos(0)):
+            self.stage[slot] = self.acc[self.block((1,) + rel), :].astype(BF16)
+            self.copy(0, slot).start()
+
+    def step(self, k):
+        for slot, rel in enumerate(self.combos(k)):
+            self.copy(k, slot).wait_recv()
+            block = self.block((0,) * (k + 1) + rel)
+            total = self.acc[block, :] + self.recv[self.base[k] + slot].astype(F32)
+            if not rel:
+                self.out[...] = total * self.scale
+            elif rel[0]:
+                later = self.combos(k + 1).index(rel[1:])
+                self.stage[self.base[k + 1] + later] = total.astype(BF16)
+                self.copy(k + 1, later).start()
+            else:
+                self.acc[block, :] = total
+
+    def finish(self):
+        for k in range(len(self.order)):
+            for slot in range(len(self.combos(k))):
+                self.copy(k, slot).wait_send()
+
+
+def fused_kernel(
+    devices, stride, scale,
+    x_ref, gain_ref, dw_ref, lw_ref, cot_ref,
+    bo_ref, ig_ref, gd_ref, gl_ref,
+    act, act_in, act_t, act_in_t, cotp, hidp, cots, d_hid, slope_in, hid_t, dmid, dmid_in,
+    acc_l, acc_d, stage_l, recv_l, stage_d, recv_d,
+    act_ss, act_rs, dm_ss, dm_rs, halo_ss, halo_rs, l_ss, l_rs, d_ss, d_rs,
+):
+    rows, width = x_ref.shape
+    chunks = rows // CHUNK
+    me = lax.axis_index("seq")
+    upper = lax.div(me, stride)
+    far = across(me, stride)
+    tap_in = 2 - 2 * upper
+    tap_out = 2 * upper
+    has_left, has_right = me > 0, me < devices - 1
+    left, right = jnp.maximum(me - 1, 0), jnp.minimum(me + 1, devices - 1)
+    bits = [1 << i for i in range(devices.bit_length() - 1)]
+
+    barrier = pltpu.get_barrier_semaphore()
+    for bit in bits:
+        pl.semaphore_signal(barrier, inc=1, device_id={"seq": across(me, bit)}, device_id_type=MESH)
+
+    @pl.when(has_left)
+    def _():
+        pl.semaphore_signal(barrier, inc=1, device_id={"seq": left}, device_id_type=MESH)
+
+    @pl.when(has_right)
+    def _():
+        pl.semaphore_signal(barrier, inc=1, device_id={"seq": right}, device_id_type=MESH)
+
+    def chunk(c):
+        return pl.ds(pl.multiple_of(c * CHUNK, CHUNK), CHUNK)
+
+    def padded_chunk(c):
+        return pl.ds(pl.multiple_of(PAD + c * CHUNK, PAD), CHUNK)
+
+    def moved(src, dst, ss, rs, c):
+        return pltpu.make_async_remote_copy(
+            src_ref=src.at[chunk(c)], dst_ref=dst.at[chunk(c)],
+            send_sem=ss.at[c], recv_sem=rs.at[c],
+            device_id={"seq": far}, device_id_type=MESH,
+        )
+
+    def to_right(buf, k):
+        return pltpu.make_async_remote_copy(
+            src_ref=buf.at[pl.ds(rows, PAD)], dst_ref=buf.at[pl.ds(0, PAD)],
+            send_sem=halo_ss.at[k], recv_sem=halo_rs.at[k],
+            device_id={"seq": right}, device_id_type=MESH,
+        )
+
+    def to_left(buf, k):
+        return pltpu.make_async_remote_copy(
+            src_ref=buf.at[pl.ds(PAD, PAD)], dst_ref=buf.at[pl.ds(rows + PAD, PAD)],
+            send_sem=halo_ss.at[k], recv_sem=halo_rs.at[k],
+            device_id={"seq": left}, device_id_type=MESH,
+        )
+
+    def halo_start(buf, k):
+        @pl.when(has_right)
+        def _():
+            to_right(buf, k).start()
+
+        @pl.when(has_left)
+        def _():
+            to_left(buf, k + 1).start()
+
+    def halo_wait(buf, k):
+        @pl.when(has_right)
+        def _():
+            to_right(buf, k).wait_send()
+            to_left(buf, k + 1).wait_recv()
+
+        @pl.when(has_left)
+        def _():
+            to_left(buf, k + 1).wait_send()
+            to_right(buf, k).wait_recv()
+
+    @pl.when(jnp.logical_not(has_left))
+    def _():
+        cotp[0:PAD, :] = jnp.zeros((PAD, width), BF16)
+        hidp[0:PAD, :] = jnp.zeros((PAD, width), BF16)
+
+    @pl.when(jnp.logical_not(has_right))
+    def _():
+        cotp[rows + PAD : rows + 2 * PAD, :] = jnp.zeros((PAD, width), BF16)
+        hidp[rows + PAD : rows + 2 * PAD, :] = jnp.zeros((PAD, width), BF16)
+
+    cotp[PAD : rows + PAD, :] = cot_ref[...]
+    pl.semaphore_wait(
+        barrier, len(bits) + has_left.astype(jnp.int32) + has_right.astype(jnp.int32)
+    )
+    halo_start(cotp, 0)
+
+    def prepare_chunk(c, _):
+        v = x_ref[chunk(c), :].astype(F32)
+        rstd = lax.rsqrt(jnp.mean(v * v, axis=-1, keepdims=True) + 1e-06)
+        a, slope = gelu_and_slope(v * rstd * gain_ref[...])
+        act[chunk(c), :] = a.astype(BF16)
+        moved(act, act_in, act_ss, act_rs, c).start()
+        slope_in[chunk(c), :] = slope * gain_ref[...]
+        return 0
+
+    lax.fori_loop(0, chunks, prepare_chunk, 0)
+    halo_wait(cotp, 0)
+
+    def cot_chunk(c, _):
+        window = cotp[pl.ds(pl.multiple_of(c * CHUNK, CHUNK), CHUNK + 2 * PAD), :].astype(F32)
+        total = jnp.zeros((CHUNK, width), F32)
+        for j in range(5):
+            shifted = window[PAD + 2 - j : PAD + 2 - j + CHUNK].astype(BF16)
+            cots[j, chunk(c), :] = shifted
+            total = total + dot_t(shifted, lw_ref[j])
+        d_hid[chunk(c), :] = total
+        act_t[:, chunk(c)] = act[chunk(c), :].astype(F32).T.astype(BF16)
+        return 0
+
+    lax.fori_loop(0, chunks, cot_chunk, 0)
+
+    def middle_chunk(c, _):
+        moved(act, act_in, act_ss, act_rs, c).wait_recv()
+        other = act_in[chunk(c), :]
+        mid = dot(act[chunk(c), :], dw_ref[1]) + dot(other, dw_ref[tap_in])
+        hid, slope = gelu_and_slope(mid)
+        dm = (d_hid[chunk(c), :] * slope).astype(BF16)
+        dmid[chunk(c), :] = dm
+        moved(dmid, dmid_in, dm_ss, dm_rs, c).start()
+        hid = hid.astype(BF16)
+        hidp[padded_chunk(c), :] = hid
+        hid_t[:, chunk(c)] = hid.astype(F32).T.astype(BF16)
+        act_in_t[:, chunk(c)] = other.astype(F32).T.astype(BF16)
+        return 0
+
+    lax.fori_loop(0, chunks, middle_chunk, 0)
+    halo_start(hidp, 2)
+
+    sum_l = HalvingSum(
+        me, bits, gl_ref.shape[0], acc_l, stage_l, recv_l, gl_ref, l_ss, l_rs, scale
+    )
+    d_order = [bits[0], bits[2], bits[1]] + bits[3:]
+    sum_d = HalvingSum(
+        me, d_order, gd_ref.shape[0], acc_d, stage_d, recv_d, gd_ref, d_ss, d_rs, scale
+    )
+
+    def local_tap(j, _):
+        acc_l[pl.ds(pl.multiple_of(j * width, width), width), :] = dot(hid_t[...], cots[j])
+        return 0
+
+    lax.fori_loop(0, 5, local_tap, 0)
+    sum_l.begin()
+    acc_d[width : 2 * width, :] = dot(act_t[...], dmid[...])
+    acc_d[pl.ds(pl.multiple_of(tap_in * width, width), width), :] = dot(act_in_t[...], dmid[...])
+    acc_d[pl.ds(pl.multiple_of(tap_out * width, width), width), :] = jnp.zeros((width, width), F32)
+    sum_d.begin()
+    sum_l.step(0)
+    sum_d.step(0)
+
+    halo_wait(hidp, 2)
+
+    def out_chunk(c, _):
+        window = hidp[pl.ds(pl.multiple_of(c * CHUNK, CHUNK), CHUNK + 2 * PAD), :].astype(F32)
+        total = x_ref[chunk(c), :].astype(F32)
+        for j in range(5):
+            total = total + dot(window[PAD - 2 + j : PAD - 2 + j + CHUNK].astype(BF16), lw_ref[j])
+        bo_ref[chunk(c), :] = total.astype(BF16)
+        return 0
+
+    lax.fori_loop(0, chunks, out_chunk, 0)
+    for k in range(1, len(bits) - 1):
+        sum_l.step(k)
+        sum_d.step(k)
+
+    def grad_chunk(c, _):
+        moved(dmid, dmid_in, dm_ss, dm_rs, c).wait_recv()
+        d_act = dot_t(dmid[chunk(c), :], dw_ref[1]) + dot_t(dmid_in[chunk(c), :], dw_ref[tap_out])
+        v = x_ref[chunk(c), :].astype(F32)
+        rstd = lax.rsqrt(jnp.mean(v * v, axis=-1, keepdims=True) + 1e-06)
+        du = d_act * slope_in[chunk(c), :]
+        unit = v * rstd
+        dv = rstd * (du - unit * jnp.mean(du * unit, axis=-1, keepdims=True))
+        ig_ref[chunk(c), :] = (cot_ref[chunk(c), :].astype(F32) + dv).astype(BF16)
+        return 0
+
+    lax.fori_loop(0, chunks, grad_chunk, 0)
+    sum_l.step(len(bits) - 1)
+    sum_d.step(len(bits) - 1)
+
+    def sent(c, _):
+        moved(act, act_in, act_ss, act_rs, c).wait_send()
+        moved(dmid, dmid_in, dm_ss, dm_rs, c).wait_send()
+        return 0
+
+    lax.fori_loop(0, chunks, sent, 0)
+    sum_l.finish()
+    sum_d.finish()
+
+
+def paired(devices, inputs, norm_gain, dilated_weight, local_weight, cotangent):
+    rows, width = inputs.shape
+    stride = DILATION_BINS // rows
+    scale = 1.0 / math.sqrt(rows * devices)
+    chunks = rows // CHUNK
+    rows_d, rows_l = 3 * width // devices, 5 * width // devices
+    vmem = pltpu.VMEM
+    dma = pltpu.SemaphoreType.DMA
+    whole = pl.BlockSpec(memory_space=pltpu.VMEM)
+    flops = 2 * rows * width * width * (5 * 3 + 2 * 3)
+    return pl.pallas_call(
+        functools.partial(fused_kernel, devices, stride, scale),
+        out_shape=(
+            jax.ShapeDtypeStruct((rows, width), BF16),
+            jax.ShapeDtypeStruct((rows, width), BF16),
+            jax.ShapeDtypeStruct((rows_d, width), F32),
+            jax.ShapeDtypeStruct((rows_l, width), F32),
+        ),
+        in_specs=[whole] * 5,
+        out_specs=(whole,) * 4,
+        scratch_shapes=[
+            vmem((rows, width), BF16),
+            vmem((rows, width), BF16),
+            vmem((width, rows), BF16),
+            vmem((width, rows), BF16),
+            vmem((rows + 2 * PAD, width), BF16),
+            vmem((rows + 2 * PAD, width), BF16),
+            vmem((5, rows, width), BF16),
+            vmem((rows, width), F32),
+            vmem((rows, width), F32),
+            vmem((width, rows), BF16),
+            vmem((rows, width), BF16),
+            vmem((rows, width), BF16),
+            vmem((5 * width, width), F32),
+            vmem((3 * width, width), F32),
+            vmem((devices - 1, rows_l, width), BF16),
+            vmem((devices - 1, rows_l, width), BF16),
+            vmem((devices - 1, rows_d, width), BF16),
+            vmem((devices - 1, rows_d, width), BF16),
+            dma((chunks,)), dma((chunks,)), dma((chunks,)), dma((chunks,)),
+            dma((4,)), dma((4,)),
+            dma((devices - 1,)), dma((devices - 1,)), dma((devices - 1,)), dma((devices - 1,)),
+        ],
+        compiler_params=pltpu.CompilerParams(
+            collective_id=0, has_side_effects=True, vmem_limit_bytes=58 * 2**20
+        ),
+        cost_estimate=pl.CostEstimate(
+            flops=flops, bytes_accessed=12 * 2**20, transcendentals=2 * rows * width
+        ),
+    )(inputs, norm_gain.reshape(1, width), dilated_weight, local_weight, cotangent)
+
+
+def pairs_up(devices, rows, width):
+    return (
+        devices >= 8
+        and devices & (devices - 1) == 0
+        and devices * rows == 2 * DILATION_BINS
+        and rows % CHUNK == 0
+        and width % (16 * devices) == 0
+    )
+
+
 def solution(mesh):
+    def body(inputs, norm_gain, dilated_weight, local_weight, cotangent):
+        arrays = (inputs, norm_gain, dilated_weight, local_weight, cotangent)
+        devices = mesh.shape["seq"]
+        if pairs_up(devices, *inputs.shape):
+            return paired(devices, *arrays)
+        return on_device(*arrays)
+
     return jax.shard_map(
-        on_device,
+        body,
         mesh=mesh,
         in_specs=(P(("groups", "seq"), None), P(), P(), P(), P(("groups", "seq"), None)),
         out_specs=(

time: 263 us -> 125 us (0.48)
  waiting for transfers between devices: 162 us -> 0 us
  Pallas kernels: 0 us -> 119 us
  matrix products: 36 us -> 0 us
  starting transfers between devices: 29 us -> 0 us
  between operations: 14.3 us -> 0.67 us
  other arithmetic: 10.9 us -> 0 us
  local copies, waits for them, and re-layouts: 7.74 us -> 4.76 us
    pallas_call x0 -> x1, Pallas kernels: none -> 119 us  [paired(): pl.pallas_call(functools.partial(fused_kernel, devices, stride, scale), o...]
    ppermute x8 -> x0, waiting for transfers between devices: 85.6 us -> none  [the longest x4 76.6 us: from_behind(): return lax.ppermute(x, axis, pairs)]
    reduce_scatter x2 -> x0, waiting for transfers between devices: 76.5 us -> none  [the longest x1 76.5 us: on_device(): lax.psum_scatter(transposed_term(hid_all, cotangent, scale), 'seq', scatt...]
    dot_general x8 -> x0, matrix products: 36 us -> none  [the longest x2 12.9 us: transposed_term(): lax.dot_general(left, right, (((0,), (0,)), ((), ())), preferred_element_...]
    ppermute x8 -> x0, starting transfers between devices: 28.9 us -> none  [the longest x4 14.5 us: from_behind(): return lax.ppermute(x, axis, pairs)]
    unnamed x4 -> x0, other arithmetic: 4.08 us -> none
    convert_element_type x2 -> x0, other arithmetic: 3.7 us -> none  [the longest x1 2.14 us: on_device(): activation_input = act_f.astype(jnp.bfloat16)]
    unnamed x20 -> x10, local copies, waits for them, and re-layouts: 7.72 us -> 4.76 us
  transfers between devices with their start and end apart: 10 -> 0, of which waited for: 5 -> 0; matrix products, arithmetic and copies ran while one was open for 15% -> 0% of each run, Pallas kernels for 0% -> 0%
where the time goes in v1:
time: 125 us
  Pallas kernels  119 us (95%)
  local copies, waits for them, and re-layouts  4.76 us (4%)
    pallas_call x1, Pallas kernels, paired(): pl.pallas_call(functools.partial(fused_kernel, devices, stride, scale), o...  119 us
    unnamed x10, local copies, waits for them, and re-layouts  4.76 us

profile of v1, /device:TPU:3, one launch (start us, length us, event | category | flops | bytes accessed | tf_op | source)
XLA Modules:
  0.0 124.8 jit_solution(129316100961968496)
XLA Ops:
  0.6 119.3 %shard_map.84 = (bf16[1024,512]{1,0:T(8,128)(2,1)}, bf16[1024,512]{1,0:T(8,128)(2,1)}, f32[96,512]{1,0:T(8,128)}, f32[160,512]{1,0:T(8,128)}) custom-call(bf16[1024,512]{1,0:T(8,128)(2,1)} %x_ref.1, f32[1,512]{1,0:T(1,128)} %bitcast.1, bf16[3,512,512]{2,1,0:T(8,128)(2,1)} %dw_ref.1, bf16[5,512,512]{2,1,0:T(8,128)(2,1)} %lw_ref.1, bf16[1024,512]{1,0:T(8,128)(2,1)} %cot_ref.1), custom_call_target="tpu_custom_call" | custom-call | flops 11274289152 | bytes 12582912 | tf_op jit(solution)/shard_map/pallas_call | solution.py:391
  120.0 0.0 copy-start
  120.0 0.0 copy-start.2
  120.0 0.0 copy-start.1
  120.0 2.4 %copy.13 = bf16[1024,512]{1,0:T(8,128)(2,1)} copy(bf16[1024,512]{1,0:T(8,128)(2,1)} %get-tuple-element.8) | data formatting | bytes 2097152
  122.4 0.0 copy-done
  122.4 1.0 copy.14
  123.4 0.0 copy-done.2
  123.4 0.7 copy.15
  124.0 0.0 copy-done.1
  124.0 0.7 copy.16
Async XLA Ops:
  120.0 2.4 %copy-start = (bf16[1024,512]{1,0:T(8,128)(2,1)S(1)}, bf16[1024,512]{1,0:T(8,128)(2,1)}, u32[]{:S(2)}) copy-start(bf16[1024,512]{1,0:T(8,128)(2,1)} %get-tuple-element.9) | copy-start | bytes 3145732
  120.0 3.4 %copy-start.2 = (f32[96,512]{1,0:T(8,128)S(1)}, f32[96,512]{1,0:T(8,128)}, u32[]{:S(2)}) copy-start(f32[96,512]{1,0:T(8,128)} %get-tuple-element.10) | copy-start | bytes 589828
  120.0 4.0 %copy-start.1 = (f32[160,512]{1,0:T(8,128)S(1)}, f32[160,512]{1,0:T(8,128)}, u32[]{:S(2)}) copy-start(f32[160,512]{1,0:T(8,128)} %get-tuple-element.11) | copy-start | bytes 983044

commit v2 on v1

--- a/solution.py
+++ b/solution.py
@@ -15,6 +15,7 @@
 GELU_B = 0.044715
 CHUNK = 128
 PAD = 16
+LAG = 4
 F32 = jnp.float32
 BF16 = jnp.bfloat16
 
@@ -183,8 +184,9 @@
 
 def fused_kernel(
     devices, stride, scale,
-    x_ref, gain_ref, dw_ref, lw_ref, cot_ref,
-    bo_ref, ig_ref, gd_ref, gl_ref,
+    x_ref, gain_ref, dw_hbm, lw_hbm, cot_ref,
+    bo_hbm, ig_hbm, gd_ref, gl_ref,
+    dw_ref, lw_ref, bo_ref, ig_ref, own_sem,
     act, act_in, act_t, act_in_t, cotp, hidp, cots, d_hid, slope_in, hid_t, dmid, dmid_in,
     acc_l, acc_d, stage_l, recv_l, stage_d, recv_d,
     act_ss, act_rs, dm_ss, dm_rs, halo_ss, halo_rs, l_ss, l_rs, d_ss, d_rs,
@@ -201,6 +203,12 @@
     bits = [1 << i for i in range(devices.bit_length() - 1)]
 
     barrier = pltpu.get_barrier_semaphore()
+    lw_in = pltpu.make_async_copy(lw_hbm, lw_ref, own_sem.at[0])
+    dw_in = pltpu.make_async_copy(dw_hbm, dw_ref, own_sem.at[1])
+    bo_out = pltpu.make_async_copy(bo_ref, bo_hbm, own_sem.at[2])
+    ig_out = pltpu.make_async_copy(ig_ref, ig_hbm, own_sem.at[3])
+    for own in (lw_in, dw_in):
+        own.start()
     for bit in bits:
         pl.semaphore_signal(barrier, inc=1, device_id={"seq": across(me, bit)}, device_id_type=MESH)
 
@@ -269,22 +277,29 @@
         cotp[rows + PAD : rows + 2 * PAD, :] = jnp.zeros((PAD, width), BF16)
         hidp[rows + PAD : rows + 2 * PAD, :] = jnp.zeros((PAD, width), BF16)
 
-    cotp[PAD : rows + PAD, :] = cot_ref[...]
-    pl.semaphore_wait(
-        barrier, len(bits) + has_left.astype(jnp.int32) + has_right.astype(jnp.int32)
-    )
-    halo_start(cotp, 0)
-
-    def prepare_chunk(c, _):
+    def prepare_chunk(c):
         v = x_ref[chunk(c), :].astype(F32)
         rstd = lax.rsqrt(jnp.mean(v * v, axis=-1, keepdims=True) + 1e-06)
         a, slope = gelu_and_slope(v * rstd * gain_ref[...])
         act[chunk(c), :] = a.astype(BF16)
+        slope_in[chunk(c), :] = slope * gain_ref[...]
+
+    cotp[PAD : rows + PAD, :] = cot_ref[...]
+    prepare_chunk(0)
+    pl.semaphore_wait(
+        barrier, len(bits) + has_left.astype(jnp.int32) + has_right.astype(jnp.int32)
+    )
+    halo_start(cotp, 0)
+    moved(act, act_in, act_ss, act_rs, 0).start()
+
+    def prepare_and_send(c, _):
+        prepare_chunk(c)
         moved(act, act_in, act_ss, act_rs, c).start()
-        slope_in[chunk(c), :] = slope * gain_ref[...]
-        return 0
-
-    lax.fori_loop(0, chunks, prepare_chunk, 0)
+        return 0
+
+    lax.fori_loop(1, chunks, prepare_and_send, 0)
+    lw_in.wait()
+    dw_in.wait()
     halo_wait(cotp, 0)
 
     def cot_chunk(c, _):
@@ -307,7 +322,11 @@
         hid, slope = gelu_and_slope(mid)
         dm = (d_hid[chunk(c), :] * slope).astype(BF16)
         dmid[chunk(c), :] = dm
-        moved(dmid, dmid_in, dm_ss, dm_rs, c).start()
+
+        @pl.when(c >= LAG)
+        def _():
+            moved(dmid, dmid_in, dm_ss, dm_rs, c - LAG).start()
+
         hid = hid.astype(BF16)
         hidp[padded_chunk(c), :] = hid
         hid_t[:, chunk(c)] = hid.astype(F32).T.astype(BF16)
@@ -317,6 +336,11 @@
     lax.fori_loop(0, chunks, middle_chunk, 0)
     halo_start(hidp, 2)
 
+    def late_send(c, _):
+        moved(dmid, dmid_in, dm_ss, dm_rs, c).start()
+        return 0
+
+
     sum_l = HalvingSum(
         me, bits, gl_ref.shape[0], acc_l, stage_l, recv_l, gl_ref, l_ss, l_rs, scale
     )
@@ -330,6 +354,7 @@
         return 0
 
     lax.fori_loop(0, 5, local_tap, 0)
+    lax.fori_loop(chunks - LAG, chunks - 2, late_send, 0)
     sum_l.begin()
     acc_d[width : 2 * width, :] = dot(act_t[...], dmid[...])
     acc_d[pl.ds(pl.multiple_of(tap_in * width, width), width), :] = dot(act_in_t[...], dmid[...])
@@ -337,6 +362,11 @@
     sum_d.begin()
     sum_l.step(0)
     sum_d.step(0)
+    lax.fori_loop(chunks - 2, chunks, late_send, 0)
+
+    for k in range(1, len(bits) - 1):
+        sum_l.step(k)
+        sum_d.step(k)
 
     halo_wait(hidp, 2)
 
@@ -349,9 +379,7 @@
         return 0
 
     lax.fori_loop(0, chunks, out_chunk, 0)
-    for k in range(1, len(bits) - 1):
-        sum_l.step(k)
-        sum_d.step(k)
+    bo_out.start()
 
     def grad_chunk(c, _):
         moved(dmid, dmid_in, dm_ss, dm_rs, c).wait_recv()
@@ -361,10 +389,11 @@
         du = d_act * slope_in[chunk(c), :]
         unit = v * rstd
         dv = rstd * (du - unit * jnp.mean(du * unit, axis=-1, keepdims=True))
-        ig_ref[chunk(c), :] = (cot_ref[chunk(c), :].astype(F32) + dv).astype(BF16)
+        ig_ref[chunk(c), :] = (cotp[padded_chunk(c), :].astype(F32) + dv).astype(BF16)
         return 0
 
     lax.fori_loop(0, chunks, grad_chunk, 0)
+    ig_out.start()
     sum_l.step(len(bits) - 1)
     sum_d.step(len(bits) - 1)
 
@@ -374,8 +403,36 @@
         return 0
 
     lax.fori_loop(0, chunks, sent, 0)
+    bo_out.wait()
+    ig_out.wait()
     sum_l.finish()
     sum_d.finish()
+
+
+def handing_kernel(*refs):
+    count = len(refs) // 3
+    sources, targets, held, sems = refs[:count], refs[count : 2 * count], refs[2 * count : -1], refs[-1]
+    ins = [pltpu.make_async_copy(sources[i], held[i], sems.at[0, i]) for i in range(count)]
+    outs = [pltpu.make_async_copy(held[i], targets[i], sems.at[1, i]) for i in range(count)]
+    for copy in ins:
+        copy.start()
+    for i in range(count):
+        ins[i].wait()
+        outs[i].start()
+    for copy in outs:
+        copy.wait()
+
+
+def handed_on(results):
+    left_out = pl.BlockSpec(memory_space=pl.ANY)
+    return pl.pallas_call(
+        handing_kernel,
+        out_shape=tuple(jax.ShapeDtypeStruct(r.shape, r.dtype) for r in results),
+        in_specs=[left_out] * len(results),
+        out_specs=(left_out,) * len(results),
+        scratch_shapes=[pltpu.VMEM(r.shape, r.dtype) for r in results]
+        + [pltpu.SemaphoreType.DMA((2, len(results)))],
+    )(*results)
 
 
 def paired(devices, inputs, norm_gain, dilated_weight, local_weight, cotangent):
@@ -387,8 +444,9 @@
     vmem = pltpu.VMEM
     dma = pltpu.SemaphoreType.DMA
     whole = pl.BlockSpec(memory_space=pltpu.VMEM)
+    left_out = pl.BlockSpec(memory_space=pl.ANY)
     flops = 2 * rows * width * width * (5 * 3 + 2 * 3)
-    return pl.pallas_call(
+    results = pl.pallas_call(
         functools.partial(fused_kernel, devices, stride, scale),
         out_shape=(
             jax.ShapeDtypeStruct((rows, width), BF16),
@@ -396,9 +454,14 @@
             jax.ShapeDtypeStruct((rows_d, width), F32),
             jax.ShapeDtypeStruct((rows_l, width), F32),
         ),
-        in_specs=[whole] * 5,
-        out_specs=(whole,) * 4,
+        in_specs=[whole, whole, left_out, left_out, whole],
+        out_specs=(left_out, left_out, whole, whole),
         scratch_shapes=[
+            vmem((3, width, width), BF16),
+            vmem((5, width, width), BF16),
+            vmem((rows, width), BF16),
+            vmem((rows, width), BF16),
+            dma((4,)),
             vmem((rows, width), BF16),
             vmem((rows, width), BF16),
             vmem((width, rows), BF16),
@@ -428,6 +491,7 @@
             flops=flops, bytes_accessed=12 * 2**20, transcendentals=2 * rows * width
         ),
     )(inputs, norm_gain.reshape(1, width), dilated_weight, local_weight, cotangent)
+    return handed_on(results)
 
 
 def pairs_up(devices, rows, width):

time: 125 us -> 115 us (0.920); the launches traced: 125 us -> 113 us
  Pallas kernels: 119 us -> 113 us
  local copies, waits for them, and re-layouts: 4.76 us -> 0 us
    pallas_call x1, Pallas kernels: 119 us -> 110 us  [paired(): pl.pallas_call(functools.partial(fused_kernel, devices, stride, scale), o...]
    unnamed x10 -> x0, local copies, waits for them, and re-layouts: 4.76 us -> none
    pallas_call x0 -> x1, Pallas kernels: none -> 2.77 us  [handed_on(): pl.pallas_call(handing_kernel, out_shape=tuple((jax.ShapeDtypeStruct(r.sh...]
where the time goes in v2:
time: 115 us; the launch traced here: 113 us
  Pallas kernels  113 us (98%)
    pallas_call x1, Pallas kernels, paired(): pl.pallas_call(functools.partial(fused_kernel, devices, stride, scale), o...  110 us
    pallas_call x1, Pallas kernels, handed_on(): pl.pallas_call(handing_kernel, out_shape=tuple((jax.ShapeDtypeStruct(r.sh...  2.77 us

profile of v2, /device:TPU:3, one launch (start us, length us, event | category | flops | bytes accessed | tf_op | source)
XLA Modules:
  0.0 113.3 jit_solution(4365754934963830659)
XLA Ops:
  0.6 109.8 %shard_map.84 = (bf16[1024,512]{1,0:T(8,128)(2,1)}, bf16[1024,512]{1,0:T(8,128)(2,1)}, f32[96,512]{1,0:T(8,128)}, f32[160,512]{1,0:T(8,128)}) custom-call(bf16[1024,512]{1,0:T(8,128)(2,1)} %x_ref.1, f32[1,512]{1,0:T(1,128)} %bitcast.1, bf16[3,512,512]{2,1,0:T(8,128)(2,1)} %dw_hbm.1, bf16[5,512,512]{2,1,0:T(8,128)(2,1)} %lw_hbm.1, bf16[1024,512]{1,0:T(8,128)(2,1)} %cot_ref.1), custom_call_target="tpu_custom_call" | custom-call | flops 11274289152 | bytes 12582912 | tf_op jit(solution)/shard_map/pallas_call | solution.py:449
  110.5 2.8 %shard_map.85 = (bf16[1024,512]{1,0:T(8,128)(2,1)}, bf16[1024,512]{1,0:T(8,128)(2,1)}, f32[96,512]{1,0:T(8,128)}, f32[160,512]{1,0:T(8,128)}) custom-call(bf16[1024,512]{1,0:T(8,128)(2,1)} %get-tuple-element.8.refs_0_, bf16[1024,512]{1,0:T(8,128)(2,1)} %get-tuple-element.9.refs_1_, f32[96,512]{1,0:T(8,128)} %get-tuple-element.10.refs_2_, ...), custom_call_target="tpu_custom_call" | custom-call | tf_op jit(solution)/shard_map/pallas_call | solution.py:428
